TPU v7x, 256 devices: a whole 4x4x8 slice. The times are simulated.
256 devices in a mesh: wide: 16 (over z_lo, y), narrow: 16 (over x, z_hi, core).
Axes of the slice: x: 4, y: 4, z: 8 (z_hi: 2, z_lo: 4; z = z_hi * 4 + z_lo), core: 2. Of those that a mesh axis runs over, the one named last changes fastest.
Arguments:
- frame_queries: bfloat16 [65536, 1536], P(('wide', 'narrow')), may hold values from -8 to 8
- frame_keys: bfloat16 [65536, 1536], P(('wide', 'narrow')), may hold values from -8 to 8
- frame_values: bfloat16 [65536, 1536], P(('wide', 'narrow')), may hold values from -6 to 6
- short_head_offsets: int32 [24], replicated, may hold values from 0 to 1
- middle_head_offsets: int32 [24], replicated, may hold values from 0 to 31
- global_head_offsets: int32 [24], replicated, may hold values from 0 to 127
- w_out: bfloat16 [1536, 1536], replicated, may hold values from -1.25 to 1.25
Outputs:
- layer_out: float32 [65536, 1536], P(('wide', 'narrow'))
All inputs are finite; a program needn't handle non-finite values.
Results may differ from a plain program's by a relative error of at most 0.0036.
Values may be sent and summed in bfloat16 or wider, within the bound.
A program may use at most 64 MiB of HBM per device.

v0:
```python
import math

import jax
import jax.numpy as jnp
from jax import lax
from jax.sharding import PartitionSpec as P

KEPT_ROWS = 512


MASKED = -1e30


def from_partner(array, axis, distance):
    return lax.ppermute(array, axis, [(i, i ^ 1 << distance) for i in range(lax.axis_size(axis))])


def select_rows(source_arr, dilation, offsets, head_number):
    frame_total, row_width = source_arr.shape
    head_dim = row_width // head_number
    lane_offsets = jnp.repeat(offsets, head_dim)
    chosen = jnp.arange(dilation, dtype=jnp.int32)[:, None] == lane_offsets[None, :]
    shaped = source_arr.reshape(frame_total // dilation, dilation, row_width)
    picked = jnp.where(chosen[None], shaped, jnp.zeros((), source_arr.dtype))
    return jnp.sum(picked, axis=1)


def attend_local(sel_query, sel_key, sel_value, head_number):
    head_dim = sel_query.shape[1] // head_number
    query_heads = sel_query.reshape(sel_query.shape[0], head_number, head_dim)
    key_heads = sel_key.reshape(sel_key.shape[0], head_number, head_dim)
    value_heads = sel_value.reshape(sel_value.shape[0], head_number, head_dim)
    scores = jnp.einsum(
        "qhd,khd->hqk", query_heads, key_heads, preferred_element_type=jnp.float32
    ) * (1.0 / math.sqrt(head_dim))
    row_peak = jnp.max(scores, axis=2, keepdims=True)
    exp_scores = jnp.exp(scores - row_peak)
    totals = jnp.sum(exp_scores, axis=2)
    numerator = jnp.einsum(
        "hqk,khd->qhd",
        exp_scores.astype(jnp.bfloat16),
        value_heads,
        preferred_element_type=jnp.float32,
    )
    scope_out = numerator / jnp.transpose(totals)[:, :, None]
    scope_lse = jnp.transpose(row_peak[:, :, 0] + jnp.log(totals))
    return (scope_out, scope_lse)


def scatter_to_frames(scope_out, scope_lse, dilation, offsets):
    row_count, head_number, head_dim = scope_out.shape
    row_width = head_number * head_dim
    lane_offsets = jnp.repeat(offsets, head_dim)
    lane_cover = jnp.arange(dilation, dtype=jnp.int32)[:, None] == lane_offsets[None, :]
    flat_out = scope_out.reshape(row_count, 1, row_width)
    full_out = jnp.where(lane_cover[None], flat_out, 0.0).reshape(row_count * dilation, row_width)
    covered = jnp.arange(dilation, dtype=jnp.int32)[:, None] == offsets[None, :]
    lse_frames = jnp.where(covered[None], scope_lse[:, None, :], MASKED).reshape(
        row_count * dilation, head_number
    )
    cover_frames = jnp.broadcast_to(covered[None], (row_count, dilation, head_number)).reshape(
        row_count * dilation, head_number
    )
    return (full_out, lse_frames, cover_frames)


def per_device(
    frame_queries,
    frame_keys,
    frame_values,
    short_head_offsets,
    middle_head_offsets,
    global_head_offsets,
    w_out,
):
    frame_total, row_width = frame_queries.shape
    head_number = short_head_offsets.shape[0]
    head_dim = row_width // head_number
    narrow_total = lax.axis_size("narrow")
    wide_total = lax.axis_size("wide")
    short_dilation = 4 * frame_total // KEPT_ROWS
    middle_dilation = 4 * narrow_total * frame_total // KEPT_ROWS
    global_dilation = wide_total * narrow_total * frame_total // KEPT_ROWS
    short_scope_query = select_rows(frame_queries, short_dilation, short_head_offsets, head_number)
    short_scope_key = select_rows(frame_keys, short_dilation, short_head_offsets, head_number)
    short_scope_value = select_rows(frame_values, short_dilation, short_head_offsets, head_number)
    middle_query = select_rows(frame_queries, middle_dilation, middle_head_offsets, head_number)
    middle_key = select_rows(frame_keys, middle_dilation, middle_head_offsets, head_number)
    middle_value = select_rows(frame_values, middle_dilation, middle_head_offsets, head_number)
    global_query = select_rows(frame_queries, global_dilation, global_head_offsets, head_number)
    global_key = select_rows(frame_keys, global_dilation, global_head_offsets, head_number)
    global_value = select_rows(frame_values, global_dilation, global_head_offsets, head_number)
    middle_key, middle_value = (
        lax.all_gather(middle_key, "narrow", axis=0, tiled=True),
        lax.all_gather(middle_value, "narrow", axis=0, tiled=True),
    )
    global_key, global_value = (
        lax.all_gather(global_key, ("wide", "narrow"), axis=0, tiled=True),
        lax.all_gather(global_value, ("wide", "narrow"), axis=0, tiled=True),
    )
    for bit_pos in range(2):
        partner = from_partner((short_scope_key, short_scope_value), "narrow", bit_pos)
        short_scope_key = jnp.concatenate([short_scope_key, partner[0]], axis=0)
        short_scope_value = jnp.concatenate([short_scope_value, partner[1]], axis=0)
    short_output, short_logsumexp = attend_local(
        short_scope_query, short_scope_key, short_scope_value, head_number
    )
    for bit_pos in range(2):
        partner = from_partner((middle_key, middle_value), "wide", bit_pos)
        middle_key = jnp.concatenate([middle_key, partner[0]], axis=0)
        middle_value = jnp.concatenate([middle_value, partner[1]], axis=0)
    middle_output, middle_logsumexp = attend_local(
        middle_query, middle_key, middle_value, head_number
    )
    global_output, global_logsumexp = attend_local(
        global_query, global_key, global_value, head_number
    )
    framed = [
        scatter_to_frames(short_output, short_logsumexp, short_dilation, short_head_offsets),
        scatter_to_frames(middle_output, middle_logsumexp, middle_dilation, middle_head_offsets),
        scatter_to_frames(global_output, global_logsumexp, global_dilation, global_head_offsets),
    ]
    stacked_lse = jnp.stack([scope_item[1] for scope_item in framed])
    stacked_cover = jnp.stack([scope_item[2] for scope_item in framed])
    any_cover = jnp.any(stacked_cover, axis=0)
    top_lse = jnp.where(any_cover, jnp.max(stacked_lse, axis=0), 0.0)
    weights = jnp.where(stacked_cover, jnp.exp(stacked_lse - top_lse[None]), 0.0)
    denominator = jnp.where(any_cover, jnp.sum(weights, axis=0), 1.0)
    accumulated = jnp.zeros((frame_total, row_width), jnp.float32)
    for position in range(3):
        accumulated = (
            accumulated + jnp.repeat(weights[position], head_dim, axis=1) * framed[position][0]
        )
    merged = (accumulated / jnp.repeat(denominator, head_dim, axis=1)).astype(jnp.bfloat16)
    return jnp.dot(merged, w_out, preferred_element_type=jnp.float32)


def solution(mesh):
    placed = (
        P(("wide", "narrow"), None),
        P(("wide", "narrow"), None),
        P(("wide", "narrow"), None),
        P(),
        P(),
        P(),
        P(),
    )
    return jax.shard_map(
        per_device,
        mesh=mesh,
        in_specs=placed,
        out_specs=P(("wide", "narrow"), None),
        check_vma=False,
    )
```

profile of v0, /device:TPU:67, one launch (start us, length us, event | category | flops | bytes accessed | tf_op | source)
XLA Modules:
  0.0 917.1 jit_solution(11364216475667085460)
XLA Ops:
  6.5 0.8 broadcast_in_dim.300
  7.7 2.3 copy.167
  10.1 1.8 copy.184
  11.9 1.8 copy.165
  13.7 11.0 %fusion.34 = (bf16[2,1536]{0,1:T(8,128)(2,1)}, bf16[2,1536]{0,1:T(8,128)(2,1)}, bf16[2,1536]{0,1:T(8,128)(2,1)}) fusion(bf16[2,128,1536]{1,0,2:T(2,128)(2,1)S(1)} %copy.167, pred[128,1536]{0,1:T(8,128)(4,1)S(1)} %iota_compare_fusion, bf16[2,128,1536]{1,0,2:T(2,128)(2,1)} %copy.184, bf16[2,128,1536]{1,0,2:T(2,128)(2,1)} %copy.165), kind=kLoop, calls=%fused_computation.42 | loop fusion | flops 2350080 | bytes 2574336 | tf_op jit(solution)/shard_map/reduce_sum | solution.py:25
  24.7 1.8 copy.168
  26.7 1.2 select_reduce_fusion.2
  27.9 31.4 %all_gather.14 = bf16[128,1536]{1,0:T(8,128)(2,1)S(1)} all-gather(bf16[8,1536]{1,0:T(8,128)(2,1)S(1)} %get-tuple-element.10), channel_id=1, replica_groups=mesh['wide'=16,'narrow'=16] {'narrow'}, dimensions={0}, use_global_device_ids=true | all-gather | bytes 417792 | tf_op jit(solution)/shard_map/all_gather | solution.py:95
  59.3 1.3 collective-permute-start.6
  60.6 27.7 %all_gather.12 = bf16[128,1536]{1,0:T(8,128)(2,1)S(1)} all-gather(bf16[8,1536]{1,0:T(8,128)(2,1)S(1)} %get-tuple-element.9), channel_id=1, replica_groups=mesh['wide'=16,'narrow'=16] {'narrow'}, dimensions={0}, use_global_device_ids=true | all-gather | bytes 417792 | tf_op jit(solution)/shard_map/all_gather | solution.py:94
  88.3 1.2 reshape.337
  89.5 1.2 reshape.348
  90.7 1.2 reshape.335
  92.1 6.8 fusion.31
  99.5 0.8 copy.185
  100.4 1.1 pad_maximum_fusion.7
  101.5 3.1 collective-permute-start.7
  104.6 1.9 pad_maximum_fusion.5
  107.2 1.5 stack_reshape.21
  108.7 1.5 stack_reshape.18
  110.3 1.5 reshape.340
  111.7 0.9 copy.159
  112.8 0.7 stack_reshape.22
  113.5 1.4 copy.175
  115.0 0.7 copy.158
  115.8 0.7 copy.157
  116.4 1.4 copy.156
  117.9 1.0 pad_maximum_fusion.6
  118.9 5.2 collective-permute-start.5
  124.1 1.0 pad_maximum_fusion.4
  125.4 1.3 pad_maximum_fusion.3
  126.7 12.1 %collective-permute-done.3 = bf16[256,1536]{1,0:T(8,128)(2,1)} collective-permute-done((bf16[256,1536]{1,0:T(8,128)(2,1)}, bf16[256,1536]{1,0:T(8,128)(2,1)}, u32[]{:S(2)}, u32[]{:S(2)}) %collective-permute-start.3) | collective-permute-done | bytes 786464 | tf_op jit(solution)/shard_map/ppermute | solution.py:15
  138.8 1.3 pad_maximum_fusion.1
  140.2 1.8 copy.181
  142.0 0.7 copy.162
  144.7 0.7 broadcast_in_dim.316
  145.4 47.0 %collective-permute-done.1 = bf16[256,1536]{1,0:T(8,128)(2,1)} collective-permute-done((bf16[256,1536]{1,0:T(8,128)(2,1)}, bf16[256,1536]{1,0:T(8,128)(2,1)}, u32[]{:S(2)}, u32[]{:S(2)}) %collective-permute-start.1) | collective-permute-done | bytes 786464 | tf_op jit(solution)/shard_map/ppermute | solution.py:15
  192.5 1.2 pad_maximum_fusion
  193.7 0.7 copy.160
  194.7 3.7 multiply_reduce_fusion
  198.6 0.8 copy-done.6
  199.5 1.2 pad_maximum_fusion.2
  200.8 1.6 copy.183
  202.4 0.7 copy.178
  203.1 3.6 fusion.1
  206.7 3.7 fusion.27
  211.1 0.7 broadcast_select_fusion.4
  211.8 1.1 select_n.130
  212.9 1.6 copy.180
  214.8 0.7 broadcast_in_dim.307
  215.6 0.7 copy.177
  216.3 0.7 copy.173
  217.0 0.7 copy.172
  217.7 269.0 %all-gather.5.cloned.1.call-done = bf16[256,2,1536]{2,1,0:T(2,128)(2,1)} async-done(((bf16[1,2,1536]{2,1,0:T(2,128)(2,1)}), bf16[256,2,1536]{2,1,0:T(2,128)(2,1)}) %all-gather.5.cloned.1.call-update) | async-done | bytes 1572880 | tf_op jit(solution)/shard_map/all_gather | solution.py:98
  486.7 4.9 reshape.346
  491.6 1.0 fusion.53
  492.7 0.7 copy-done.23
  493.6 397.8 %all-gather.7.cloned.1.call-done = bf16[256,2,1536]{2,1,0:T(2,128)(2,1)} async-done(((bf16[1,2,1536]{2,1,0:T(2,128)(2,1)}), bf16[256,2,1536]{2,1,0:T(2,128)(2,1)}) %all-gather.7.cloned.1.call-update) | async-done | bytes 1572880 | tf_op jit(solution)/shard_map/all_gather | solution.py:99
  891.4 5.2 reshape.355
  896.6 0.7 fusion.24
  897.3 1.2 copy.191
  898.6 4.5 broadcast_select_fusion
  903.6 1.8 fusion.12
  905.4 4.9 fusion.55
  (159 shorter events, 6.9 us)
Async XLA Ops:
  6.5 3.5 copy-start.1
  6.5 480.2 %all-gather.5.cloned.1.call-start = ((), (), s32[]{:S(2)}) async-start(), calls=%async_computation | async-start | bytes 1579008 | tf_op jit(solution)/shard_map/all_gather | solution.py:98
  7.7 6.0 copy-start.10
  7.7 4.2 copy-start.2
  13.7 12.9 %copy-start.47 = (s32[24]{0:T(128)S(1)}, s32[24]{0:T(128)}, u32[]{:S(2)}) copy-start(s32[24]{0:T(128)} %param.11) | copy-start | bytes 292
  13.7 13.0 %copy-start = (bf16[256,1536]{1,0:T(8,128)(2,1)S(1)}, bf16[256,1536]{1,0:T(8,128)(2,1)}, u32[]{:S(2)}) copy-start(bf16[256,1536]{1,0:T(8,128)(2,1)} %param.8) | copy-start | bytes 2359300
  26.5 864.9 %all-gather.7.cloned.1.call-start = ((), (), s32[]{:S(2)}) async-start(), calls=%async_computation.1 | async-start | bytes 1579008 | tf_op jit(solution)/shard_map/all_gather | solution.py:99
  26.7 61.6 %copy-start.21 = (pred[32,1536]{1,0:T(8,128)(4,1)}, pred[32,1536]{1,0:T(8,128)(4,1)S(1)}, u32[]{:S(2)}) copy-start(pred[32,1536]{1,0:T(8,128)(4,1)S(1)} %iota_compare_fusion.1) | copy-start | bytes 147460
  59.3 41.1 %collective-permute-start.6 = (bf16[128,1536]{1,0:T(8,128)(2,1)S(1)}, bf16[128,1536]{1,0:T(8,128)(2,1)}, u32[]{:S(2)}, u32[]{:S(2)}) collective-permute-start(bf16[128,1536]{1,0:T(8,128)(2,1)S(1)} %all_gather.14), channel_id=1, source_target_pairs={{0,16},{16,0},{32,48},{48,32},{64,80},{80,64},{96,112},{112,96},{1... | collective-permute-start | bytes 1179656 | tf_op jit(solution)/shard_map/ppermute | solution.py:15
  88.3 16.3 %collective-permute-start.2 = (bf16[128,1536]{1,0:T(8,128)(2,1)S(1)}, bf16[128,1536]{1,0:T(8,128)(2,1)}, u32[]{:S(2)}, u32[]{:S(2)}) collective-permute-start(bf16[128,1536]{1,0:T(8,128)(2,1)S(1)} %all_gather.12), channel_id=1, source_target_pairs={{0,16},{16,0},{32,48},{48,32},{64,80},{80,64},{96,112},{112,96},{1... | collective-permute-start | bytes 1179656 | tf_op jit(solution)/shard_map/ppermute | solution.py:15
  89.5 2.4 copy-start.49
  89.5 2.6 copy-start.9
  92.1 6.9 copy-start.40
  92.1 7.4 copy-start.18
  92.1 8.2 copy-start.48
  98.9 18.9 %copy-start.5 = (bf16[128,1536]{1,0:T(8,128)(2,1)}, bf16[128,1536]{1,0:T(8,128)(2,1)S(1)}, u32[]{:S(2)}) copy-start(bf16[128,1536]{1,0:T(8,128)(2,1)S(1)} %get-tuple-element.12) | copy-start | bytes 1179652
  98.9 25.1 %copy-start.7 = (bf16[128,1536]{1,0:T(8,128)(2,1)}, bf16[128,1536]{1,0:T(8,128)(2,1)S(1)}, u32[]{:S(2)}) copy-start(bf16[128,1536]{1,0:T(8,128)(2,1)S(1)} %get-tuple-element.11) | copy-start | bytes 1179652
  99.0 18.9 %collective-permute-start.4 = (bf16[128,1536]{1,0:T(8,128)(2,1)S(1)}, bf16[128,1536]{1,0:T(8,128)(2,1)S(1)}, u32[]{:S(2)}, u32[]{:S(2)}) collective-permute-start(bf16[128,1536]{1,0:T(8,128)(2,1)S(1)} %get-tuple-element.12), channel_id=1, source_target_pairs={{0,1},{1,0},{2,3},{3,2},{4,5},{5,4},{6,7},{7,6},{8,9},{9,8},{10,11... | collective-permute-start | bytes 1179656 | tf_op jit(solution)/shard_map/ppermute | solution.py:15
  99.3 24.8 %collective-permute-start = (bf16[128,1536]{1,0:T(8,128)(2,1)S(1)}, bf16[128,1536]{1,0:T(8,128)(2,1)S(1)}, u32[]{:S(2)}, u32[]{:S(2)}) collective-permute-start(bf16[128,1536]{1,0:T(8,128)(2,1)S(1)} %get-tuple-element.11), channel_id=1, source_target_pairs={{0,1},{1,0},{2,3},{3,2},{4,5},{5,4},{6,7},{7,6},{8,9},{9,8},{10,11... | collective-permute-start | bytes 1179656 | tf_op jit(solution)/shard_map/ppermute | solution.py:15
  100.4 6.1 copy-start.50
  100.4 11.3 %copy-start.20 = (bf16[128,1536]{1,0:T(8,128)(2,1)S(1)}, bf16[128,1536]{1,0:T(8,128)(2,1)}, u32[]{:S(2)}) copy-start(bf16[128,1536]{1,0:T(8,128)(2,1)} %get-tuple-element.13) | copy-start | bytes 1179652
  101.5 23.8 %collective-permute-start.7 = (bf16[256,1536]{1,0:T(8,128)(2,1)S(1)}, bf16[256,1536]{1,0:T(8,128)(2,1)}, u32[]{:S(2)}, u32[]{:S(2)}) collective-permute-start(bf16[256,1536]{1,0:T(8,128)(2,1)S(1)} %pad_maximum_fusion.7), channel_id=1, source_target_pairs={{0,32},{16,48},{32,0},{48,16},{64,96},{80,112},{96,64},{112,80},{1... | collective-permute-start | bytes 2359304 | tf_op jit(solution)/shard_map/ppermute | solution.py:15
  106.5 32.3 %collective-permute-start.3 = (bf16[256,1536]{1,0:T(8,128)(2,1)}, bf16[256,1536]{1,0:T(8,128)(2,1)}, u32[]{:S(2)}, u32[]{:S(2)}) collective-permute-start(bf16[256,1536]{1,0:T(8,128)(2,1)} %pad_maximum_fusion.5), channel_id=1, source_target_pairs={{0,32},{16,48},{32,0},{48,16},{64,96},{80,112},{96,64},{112,80},{1... | collective-permute-start | bytes 2359304 | tf_op jit(solution)/shard_map/ppermute | solution.py:15
  115.0 10.1 %copy-start.26 = (pred[2,128,24]{2,1,0:T(8,128)(4,1)}, pred[2,128,24]{2,1,0:T(8,128)(4,1)S(1)}, u32[]{:S(2)}) copy-start(pred[2,128,24]{2,1,0:T(8,128)(4,1)S(1)} %broadcast_in_dim.288.clone) | copy-start | bytes 18436
  115.7 9.4 %copy-start.28 = (pred[8,32,24]{2,1,0:T(8,128)(4,1)}, pred[8,32,24]{2,1,0:T(8,128)(4,1)S(1)}, u32[]{:S(2)}) copy-start(pred[8,32,24]{2,1,0:T(8,128)(4,1)S(1)} %broadcast_in_dim.287.clone) | copy-start | bytes 18436
  117.9 7.2 copy-start.14
  118.9 79.7 %collective-permute-start.5 = (bf16[256,1536]{1,0:T(8,128)(2,1)}, bf16[256,1536]{1,0:T(8,128)(2,1)}, u32[]{:S(2)}, u32[]{:S(2)}) collective-permute-start(bf16[256,1536]{1,0:T(8,128)(2,1)} %pad_maximum_fusion.6), channel_id=1, source_target_pairs={{0,2},{1,3},{2,0},{3,1},{4,6},{5,7},{6,4},{7,5},{8,10},{9,11},{10,... | collective-permute-start | bytes 2359304 | tf_op jit(solution)/shard_map/ppermute | solution.py:15
  124.1 1.3 copy-start.16
  125.1 67.4 %collective-permute-start.1 = (bf16[256,1536]{1,0:T(8,128)(2,1)}, bf16[256,1536]{1,0:T(8,128)(2,1)}, u32[]{:S(2)}, u32[]{:S(2)}) collective-permute-start(bf16[256,1536]{1,0:T(8,128)(2,1)} %pad_maximum_fusion.4), channel_id=1, source_target_pairs={{0,2},{1,3},{2,0},{3,1},{4,6},{5,7},{6,4},{7,5},{8,10},{9,11},{10,... | collective-permute-start | bytes 2359304 | tf_op jit(solution)/shard_map/ppermute | solution.py:15
  142.0 0.8 copy-start.31
  142.7 1.4 copy-start.13
  143.2 2.2 copy-start.32
  143.2 49.3 %copy-start.8 = (bf16[128,1536]{1,0:T(8,128)(2,1)S(1)}, bf16[128,1536]{1,0:T(8,128)(2,1)}, u32[]{:S(2)}) copy-start(bf16[128,1536]{1,0:T(8,128)(2,1)} %copy-done.7) | copy-start | bytes 1179652
  143.2 49.3 %copy-start.17 = (bf16[128,1536]{1,0:T(8,128)(2,1)S(1)}, bf16[128,1536]{1,0:T(8,128)(2,1)}, u32[]{:S(2)}) copy-start(bf16[128,1536]{1,0:T(8,128)(2,1)} %copy-done.16) | copy-start | bytes 1179652
  143.4 0.6 copy-start.42
  193.7 1.0 copy-start.12
  194.7 3.7 copy-start.22
  194.7 3.7 copy-start.30
  198.4 1.0 copy-start.6
  198.4 1.1 copy-start.15
  210.4 0.7 copy-start.41
  212.9 1.7 copy-start.33
  212.9 1.7 copy-start.43
  212.9 3.4 copy-start.29
  212.9 4.1 copy-start.25
  217.7 273.9 %copy-start.19 = (bf16[2,1536]{0,1:T(8,128)(2,1)S(1)}, bf16[2,1536]{0,1:T(8,128)(2,1)}, u32[]{:S(2)}) copy-start(bf16[2,1536]{0,1:T(8,128)(2,1)} %get-tuple-element.7) | copy-start | bytes 18436
  492.7 0.7 copy-start.23
  493.6 403.0 %copy-start.24 = (f32[24,2,512]{2,1,0:T(2,128)S(1)}, f32[24,2,512]{2,1,0:T(2,128)}, u32[]{:S(2)}) copy-start(f32[24,2,512]{2,1,0:T(2,128)} %copy-done.23) | copy-start | bytes 294916
  896.6 1.9 copy-start.11
  896.6 6.8 copy-start.38
  896.6 6.8 copy-start.39
  897.3 5.9 copy-start.27
  897.3 6.1 copy-start.37
  898.5 4.9 copy-start.35
  898.5 4.9 copy-start.34
  898.5 4.9 copy-start.36
  898.5 4.9 copy-start.44
  898.6 4.9 copy-start.45
  898.6 4.9 copy-start.46
  898.6 5.0 copy-start.3
  898.6 5.0 copy-start.4
Sparse Core Ops, SparseCore 0:
  26.6 460.0 all-gather.4
  488.6 402.7 all-gather.6
where the time goes:
time: 929 us; the launch traced here: 917 us
  waiting for transfers between devices  726 us (78%)
  blocking collectives  59.1 us (6%)
  local copies, waits for them, and re-layouts  51.5 us (6%)
  other arithmetic  41 us (4%)
  matrix products  15 us (2%)
  between operations  14.1 us (2%)
  starting transfers between devices  10.4 us (1%)
    all_gather x1, waiting for transfers between devices, per_device(): lax.all_gather(global_value, ('wide', 'narrow'), axis=0, tiled=True)  398 us
    all_gather x1, waiting for transfers between devices, per_device(): lax.all_gather(global_key, ('wide', 'narrow'), axis=0, tiled=True)  269 us
    ppermute x8, waiting for transfers between devices, from_partner(): lax.ppermute(array, axis, [(i, i ^ 1 << distance) for i in range(lax.axis...  59.2 us
    all_gather x1, blocking collectives, per_device(): lax.all_gather(middle_value, 'narrow', axis=0, tiled=True)  31.4 us
    all_gather x1, blocking collectives, per_device(): lax.all_gather(middle_key, 'narrow', axis=0, tiled=True)  27.7 us
    reduce_sum x3, other arithmetic, select_rows(): return jnp.sum(picked, axis=1)  19 us
  transfers between devices with their start and end apart: 10, of which 4 were waited for; matrix products, arithmetic and copies ran while one was open for 7% of the time, Pallas kernels for 0%

commit v1 on v0

v1 whole, which is shorter than its diff:
```python
import math

import jax
import jax.numpy as jnp
from jax import lax
from jax.experimental import pallas as pl
from jax.experimental.pallas import tpu as pltpu
from jax.sharding import PartitionSpec as P

MESH = pl.DeviceIdType.MESH
F32 = jnp.float32
BF16 = jnp.bfloat16

LANES = 128
HEAD_DIM = 64
TILES = 12
GROUPS = 4
GROUP_TILES = TILES // GROUPS
X_CHIPS, Y_CHIPS, Z_CHIPS = 4, 4, 8
FRAMES = 256
SHORT_ROWS, MIDDLE_ROWS, GLOBAL_ROWS = 128, 8, 2
KEPT_ROWS = 512
PACKET = 32
SENDERS = 8
AHEAD = 3
X_TILE, MERGE_TILE, FINISH_TILE = 3, 5, 6
MASKED = -1e30

SIBLING, ACROSS, PASSED_ON, PACKETS, ALONG_Z, ALONG_X, RESULTS = range(7)


def first_head():
    return lax.broadcasted_iota(jnp.int32, (1, LANES), 1) < HEAD_DIM


def attend(query, key, value):
    rows = query.shape[0]
    first = first_head()
    low = first.astype(F32).astype(BF16)
    high = (1.0 - first.astype(F32)).astype(BF16)
    stacked = jnp.concatenate([query * low, query * high], axis=0)
    scores = lax.dot_general(
        stacked, key, (((1,), (1,)), ((), ())), preferred_element_type=F32
    ) * (1.0 / math.sqrt(HEAD_DIM))
    peak = jnp.max(scores, axis=1, keepdims=True)
    exps = jnp.exp(scores - peak)
    total = jnp.sum(exps, axis=1, keepdims=True)
    numerator = jnp.dot(exps.astype(BF16), value, preferred_element_type=F32)
    output = numerator / total
    spread = jnp.broadcast_to(peak + jnp.log(total), (2 * rows, LANES))
    return (
        jnp.where(first, output[:rows], output[rows:]),
        jnp.where(first, spread[:rows], spread[rows:]),
    )


def kernel(
    short_hbm, middle_hbm, global_hbm, q_hbm, k_hbm, v_hbm, w_hbm, o_ref, short_off, middle_off, global_off,
    q_in, k_in, v_in, w_in, plain, short_q, short_kv, short_out, packets, collected, role_q, gathered,
    role_out, results, merged, load_sem, send_sem, recv_sem,
):
    wide, narrow = lax.axis_index("wide"), lax.axis_index("narrow")
    x, y, c = narrow // 4, lax.rem(wide, 4), lax.rem(narrow, 2)
    z_hi, z_lo = lax.rem(narrow // 2, 2), wide // 4
    z = z_hi * 4 + z_lo
    me = y * 2 + c

    def device(dx=0, dy=0, dz=0, dc=0):
        to_z = lax.rem(z + dz, Z_CHIPS)
        return {
            "wide": lax.rem(to_z, 4) * 4 + lax.rem(y + dy, Y_CHIPS),
            "narrow": lax.rem(x + dx, X_CHIPS) * 4 + to_z // 4 * 2 + lax.rem(c + dc, 2),
        }

    def send(source, target, kind, number, to):
        return pltpu.make_async_remote_copy(
            src_ref=source, dst_ref=target, send_sem=send_sem.at[kind, number], recv_sem=recv_sem.at[kind, number],
            device_id=to, device_id_type=MESH,
        )

    def to_sibling(i):
        return send(short_kv.at[i, 0], short_kv.at[i, 1], SIBLING, i, device(dc=1))

    def across(i):
        return send(short_kv.at[i, 0], short_kv.at[i, 2], ACROSS, i, device(dz=4))

    def pass_on(i):
        return send(short_kv.at[i, 2], short_kv.at[i, 3], PASSED_ON, i, device(dc=1))

    group = [(dy, dc) for dy in range(Y_CHIPS) for dc in range(2) if dy or dc]

    def packet_to(number):
        dy, dc = group[number]
        to_y = lax.rem(y + dy, Y_CHIPS)
        return send(
            packets.at[pl.ds(to_y * GROUP_TILES, GROUP_TILES)], collected.at[me], PACKETS, number, device(dy=dy, dc=dc)
        )

    def result_to(number):
        dy, dc = group[number]
        sender = lax.rem(y + dy, Y_CHIPS) * 2 + lax.rem(c + dc, 2)
        return send(
            role_out.at[sender], results.at[c, pl.ds(y * GROUP_TILES, GROUP_TILES)], RESULTS, number, device(dy=dy, dc=dc)
        )

    def middle_along_z():
        part = gathered.at[x, :, :, pl.ds(z_hi * 64, 64)]
        return send(part, part, ALONG_Z, 4, device(dz=4))

    def global_along_z(dz):
        part = gathered.at[x, :, :, pl.ds(z * 16, 16)]
        return send(part, part, ALONG_Z, dz, device(dz=dz))

    def along_x(dx):
        return send(gathered.at[x], gathered.at[x], ALONG_X, dx, device(dx=dx))

    barrier = pltpu.get_barrier_semaphore()
    partners = [dict(dy=dy, dc=dc) for dy, dc in group]
    partners += [dict(dx=dx) for dx in range(1, X_CHIPS)]
    partners += [dict(dz=dz) for dz in range(1, Z_CHIPS)]
    for partner in partners:
        pl.semaphore_signal(barrier, inc=1, device_id=device(**partner), device_id_type=MESH)

    loads = [
        pltpu.make_async_copy(source, target, load_sem.at[number])
        for number, (source, target) in enumerate((
            (short_hbm, short_off), (middle_hbm, middle_off), (global_hbm, global_off),
            (k_hbm, k_in), (v_hbm, v_in), (q_hbm, q_in), (w_hbm, w_in),
        ))
    ]
    for load in loads:
        load.start()

    first = first_head()

    def offsets(ref, i):
        return jnp.where(first, ref[2 * i], ref[2 * i + 1])

    def select_short(source, number, i):
        lanes = pl.ds(pl.multiple_of(i * LANES, LANES), LANES)
        plain[number] = source[:, lanes].astype(F32)
        even = plain[number, pl.ds(0, SHORT_ROWS, stride=2), :]
        odd = plain[number, pl.ds(1, SHORT_ROWS, stride=2), :]
        return jnp.where(offsets(short_off, i) == 0, even, odd).astype(BF16)

    for load in loads[:5]:
        load.wait()

    @pl.loop(0, TILES)
    def _(i):
        short_kv[i, 0, 0] = select_short(k_in, 0, i)
        short_kv[i, 0, 1] = select_short(v_in, 1, i)

    pl.semaphore_wait(barrier, len(partners))

    @pl.loop(0, AHEAD)
    def _(i):
        across(i).start()

    loads[5].wait()

    @pl.loop(0, TILES)
    def _(i):
        lanes = pl.ds(pl.multiple_of(i * LANES, LANES), LANES)
        to_sibling(i).start()
        middle_at = offsets(middle_off, i)
        global_at = offsets(global_off, i)
        frame = lax.broadcasted_iota(jnp.int32, (FRAMES, LANES), 0)
        in_middle = lax.rem(frame, 32) == middle_at
        in_global = lax.rem(frame, 128) == global_at
        eight = lax.broadcasted_iota(jnp.int32, (8, LANES), 0)
        rows = []
        last = jnp.zeros((8, LANES), F32)
        for number, source in enumerate((q_in, k_in, v_in)):
            values = source[:, lanes].astype(F32)
            rows.append(jnp.sum(jnp.where(in_middle, values, 0.0).reshape(MIDDLE_ROWS, 32, LANES), axis=1))
            global_rows = jnp.sum(jnp.where(in_global, values, 0.0).reshape(GLOBAL_ROWS, 128, LANES), axis=1)
            for row in range(GLOBAL_ROWS):
                last = jnp.where(eight == 2 * number + row, global_rows[row : row + 1], last)
        packets[i] = jnp.concatenate([*rows, last], axis=0).astype(BF16)

    for number in range(len(group)):
        packet_to(number).start()
    collected[me] = packets[pl.ds(y * GROUP_TILES, GROUP_TILES)]

    @pl.loop(0, TILES)
    def _(i):
        short_q[i] = select_short(q_in, 2, i)

    o_ref[...] = jnp.zeros_like(o_ref)

    for number in range(len(group)):
        packet_to(number).wait_recv()

    def pick(row_total, place):
        row = lax.broadcasted_iota(jnp.int32, (row_total, SENDERS * PACKET), 0)
        column = lax.broadcasted_iota(jnp.int32, (row_total, SENDERS * PACKET), 1)
        return jnp.where(column == place(row), 1.0, 0.0).astype(BF16)

    def take(one_hot, tile):
        rows = collected[:, tile].reshape(SENDERS * PACKET, LANES)
        return jnp.dot(one_hot, rows, preferred_element_type=F32).astype(BF16)

    @pl.when(c == 0)
    def _():
        def place(first_row):
            return lambda row: row // 8 * PACKET + first_row + lax.rem(row, 8)

        picks = [pick(64, place(first_row)) for first_row in (0, 8, 16)]
        for tile in range(GROUP_TILES):
            role_q[tile] = take(picks[0], tile)
            for part in range(2):
                gathered[x, tile, part, pl.ds(z_hi * 64, 64), :] = take(picks[1 + part], tile)
        middle_along_z().start()

    @pl.when(c == 1)
    def _():
        def place_query(row):
            within = lax.rem(row, 8)
            return jnp.where(within < GLOBAL_ROWS, row // 8 * PACKET + 24 + within, -1)

        def place(first_row):
            return lambda row: row // 2 * PACKET + first_row + lax.rem(row, 2)

        picks = [pick(64, place_query)] + [pick(16, place(first_row)) for first_row in (26, 28)]
        for tile in range(GROUP_TILES):
            role_q[tile] = take(picks[0], tile)
            for part in range(2):
                gathered[x, tile, part, pl.ds(z * 16, 16), :] = take(picks[1 + part], tile)
        for dz in range(1, Z_CHIPS):
            global_along_z(dz).start()

    @pl.loop(AHEAD, TILES)
    def _(i):
        across(i).start()

    def short_scope(i):
        across(i).wait_recv()
        pass_on(i).start()
        to_sibling(i).wait_recv()
        pass_on(i).wait_recv()
        output, spread = attend(
            short_q[i],
            short_kv[i, :, 0].reshape(KEPT_ROWS, LANES),
            short_kv[i, :, 1].reshape(KEPT_ROWS, LANES),
        )
        short_out[i, 0] = output
        short_out[i, 1] = spread

    def finish(i):
        short_at, middle_at, global_at = (offsets(ref, i) for ref in (short_off, middle_off, global_off))
        for parity in range(2):
            shape = (SHORT_ROWS, LANES)
            row = lax.broadcasted_iota(jnp.int32, shape, 0)
            covers = (
                jnp.broadcast_to(short_at == parity, shape),
                2 * lax.rem(row, 16) + parity == middle_at,
                2 * lax.rem(row, 64) + parity == global_at,
            )

            def spread_out(value, count):
                return jnp.broadcast_to(
                    value[:count].reshape(count, 1, LANES), (count, SHORT_ROWS // count, LANES)
                ).reshape(shape)

            outs = (
                short_out[i, 0],
                spread_out(results[0, i, 0], MIDDLE_ROWS),
                spread_out(results[1, i, 0], GLOBAL_ROWS),
            )
            spreads = (
                short_out[i, 1],
                spread_out(results[0, i, 1], MIDDLE_ROWS),
                spread_out(results[1, i, 1], GLOBAL_ROWS),
            )
            masked = [jnp.where(cover, value, MASKED) for cover, value in zip(covers, spreads)]
            top = jnp.maximum(jnp.maximum(masked[0], masked[1]), masked[2])
            weights = [jnp.where(cover, jnp.exp(value - top), 0.0) for cover, value in zip(covers, masked)]
            denominator = weights[0] + weights[1] + weights[2]
            denominator = jnp.where(denominator == 0.0, 1.0, denominator)
            total = weights[0] * outs[0] + weights[1] * outs[1] + weights[2] * outs[2]
            merged[pl.ds(parity, SHORT_ROWS, stride=2), :] = total / denominator
        rows = merged[...].astype(BF16)
        depth = pl.ds(pl.multiple_of(i * LANES, LANES), LANES)
        for part in range(3):
            columns = pl.ds(part * 512, 512)
            o_ref[:, columns] += jnp.dot(rows, w_in[depth, columns], preferred_element_type=F32)

    @pl.loop(0, TILES)
    def _(i):
        @pl.when(i == X_TILE)
        def _():
            @pl.when(c == 0)
            def _():
                middle_along_z().wait_recv()

            @pl.when(c == 1)
            def _():
                for dz in range(1, Z_CHIPS):
                    global_along_z(dz).wait_recv()

            for dx in range(1, X_CHIPS):
                along_x(dx).start()

        @pl.when(i == MERGE_TILE)
        def _():
            for dx in range(1, X_CHIPS):
                along_x(dx).wait_recv()

            for tile in range(GROUP_TILES):
                output, spread = attend(
                    role_q[tile],
                    gathered[:, tile, 0].reshape(KEPT_ROWS, LANES),
                    gathered[:, tile, 1].reshape(KEPT_ROWS, LANES),
                )
                role_out[:, tile, 0] = output.reshape(SENDERS, 8, LANES)
                role_out[:, tile, 1] = spread.reshape(SENDERS, 8, LANES)
            for number in range(len(group)):
                result_to(number).start()
            results[c, pl.ds(y * GROUP_TILES, GROUP_TILES)] = role_out[me]

        short_scope(i)

        @pl.when(i == FINISH_TILE)
        def _():
            for number in range(len(group)):
                result_to(number).wait_recv()
            loads[6].wait()

        @pl.when(i >= FINISH_TILE)
        def _():
            @pl.loop(jnp.where(i == FINISH_TILE, 0, i), i + 1)
            def _(tile):
                finish(tile)

    @pl.loop(0, TILES)
    def _(i):
        to_sibling(i).wait_send()
        across(i).wait_send()
        pass_on(i).wait_send()

    for number in range(len(group)):
        packet_to(number).wait_send()
        result_to(number).wait_send()
    for dx in range(1, X_CHIPS):
        along_x(dx).wait_send()

    @pl.when(c == 0)
    def _():
        middle_along_z().wait_send()

    @pl.when(c == 1)
    def _():
        for dz in range(1, Z_CHIPS):
            global_along_z(dz).wait_send()


def per_device(queries, keys, values, short_offsets, middle_offsets, global_offsets, w_out):
    frames, width = queries.shape
    heads = short_offsets.shape
    return pl.pallas_call(
        kernel,
        out_shape=jax.ShapeDtypeStruct((frames, width), F32),
        in_specs=[pl.BlockSpec(memory_space=pltpu.HBM)] * 7,
        out_specs=pl.BlockSpec(memory_space=pltpu.VMEM),
        scratch_shapes=[
            pltpu.SMEM(heads, jnp.int32),
            pltpu.SMEM(heads, jnp.int32),
            pltpu.SMEM(heads, jnp.int32),
            pltpu.VMEM((frames, width), BF16),
            pltpu.VMEM((frames, width), BF16),
            pltpu.VMEM((frames, width), BF16),
            pltpu.VMEM((width, width), BF16),
            pltpu.VMEM((3, frames, LANES), F32),
            pltpu.VMEM((TILES, SHORT_ROWS, LANES), BF16),
            pltpu.VMEM((TILES, 4, 2, SHORT_ROWS, LANES), BF16),
            pltpu.VMEM((TILES, 2, SHORT_ROWS, LANES), F32),
            pltpu.VMEM((TILES, PACKET, LANES), BF16),
            pltpu.VMEM((SENDERS, GROUP_TILES, PACKET, LANES), BF16),
            pltpu.VMEM((GROUP_TILES, 64, LANES), BF16),
            pltpu.VMEM((X_CHIPS, GROUP_TILES, 2, 128, LANES), BF16),
            pltpu.VMEM((SENDERS, GROUP_TILES, 2, 8, LANES), F32),
            pltpu.VMEM((2, TILES, 2, 8, LANES), F32),
            pltpu.VMEM((frames, LANES), F32),
            pltpu.SemaphoreType.DMA((7,)),
            pltpu.SemaphoreType.DMA((7, TILES)),
            pltpu.SemaphoreType.DMA((7, TILES)),
        ],
        compiler_params=pltpu.CompilerParams(
            collective_id=0, has_side_effects=True, vmem_limit_bytes=60 * 1024 * 1024
        ),
        name="dilated_attention",
    )(short_offsets, middle_offsets, global_offsets, queries, keys, values, w_out)


def solution(mesh):
    placed = (
        P(("wide", "narrow"), None),
        P(("wide", "narrow"), None),
        P(("wide", "narrow"), None),
        P(),
        P(),
        P(),
        P(),
    )
    return jax.shard_map(
        per_device,
        mesh=mesh,
        in_specs=placed,
        out_specs=P(("wide", "narrow"), None),
        check_vma=False,
    )
```

time: 929 us -> 80.4 us (0.09)
  the two profiles are of different devices: /device:TPU:67 before, /device:TPU:1 now
where the time goes in v1:
time: 80.4 us; the launch traced here: 80.3 us
  Pallas kernels  77.7 us (97%)
  local copies, waits for them, and re-layouts  2.66 us (3%)
    pallas_call x1, Pallas kernels, per_device(): pl.pallas_call(kernel, out_shape=jax.ShapeDtypeStruct((frames, width), F3...  77.7 us
    unnamed x1, local copies, waits for them, and re-layouts  2.66 us

profile of v1, /device:TPU:1, one launch (start us, length us, event | category | flops | bytes accessed | tf_op | source)
XLA Modules:
  0.0 80.3 jit_solution(8820403630150040411)
XLA Ops:
  0.0 77.7 %dilated_attention.1 = f32[256,1536]{1,0:T(8,128)} custom-call(s32[24]{0:T(128)} %short_hbm.1, s32[24]{0:T(128)} %middle_hbm.1, s32[24]{0:T(128)} %global_hbm.1, bf16[256,1536]{1,0:T(8,128)(2,1)} %q_hbm.1, bf16[256,1536]{1,0:T(8,128)(2,1)} %k_hbm.1, bf16[256,1536]{1,0:T(8,128)(2,1)} %v_hbm.1, bf16[1536,1536]{1,0:T(8,128)(2,1)} %w_hbm.1), custom_call_target="tpu_custom_call" | custom-call | tf_op jit(solution)/shard_map/dilated_attention/pallas_call | solution.py:361
  77.7 2.7 %copy.9 = f32[256,1536]{1,0:T(8,128)} copy(f32[256,1536]{1,0:T(8,128)} %dilated_attention.1) | data formatting | bytes 3145728

commit v2 on v1

v2 whole, which is shorter than its diff:
```python
import math

import jax
import jax.numpy as jnp
from jax import lax
from jax.experimental import pallas as pl
from jax.experimental.pallas import tpu as pltpu
from jax.sharding import PartitionSpec as P

MESH = pl.DeviceIdType.MESH
F32 = jnp.float32
BF16 = jnp.bfloat16

LANES = 128
HEAD_DIM = 64
TILES = 12
X_CHIPS, Y_CHIPS, Z_CHIPS = 4, 4, 8
CHIPS = X_CHIPS * Y_CHIPS
PLANE = 2 * CHIPS
FRAMES = 256
SHORT_ROWS, MIDDLE_ROWS, GLOBAL_ROWS = 128, 8, 2
KEPT_ROWS = 512
MIDDLE_PACKET = 32
GLOBAL_PACKET = 16
BLOCK = 8
BLOCKS = PLANE // BLOCK
GLOBAL_SHIFT = 4
AHEAD = 6
FINISH_TILE = 6
PROJECTED = (0, FINISH_TILE, 9, 11, 12)
MASKED = -1e30

SIBLING, ACROSS, PASSED_ON, ALONG_Z = range(4)


def first_head():
    return lax.broadcasted_iota(jnp.int32, (1, LANES), 1) < HEAD_DIM


def attend(query, key, value):
    rows = query.shape[0]
    first = first_head()
    low = first.astype(F32).astype(BF16)
    high = (1.0 - first.astype(F32)).astype(BF16)
    stacked = jnp.concatenate([query * low, query * high], axis=0)
    scores = lax.dot_general(
        stacked, key, (((1,), (1,)), ((), ())), preferred_element_type=F32
    ) * (1.0 / math.sqrt(HEAD_DIM))
    peak = jnp.max(scores, axis=1, keepdims=True)
    exps = jnp.exp(scores - peak)
    total = jnp.sum(exps, axis=1, keepdims=True)
    numerator = jnp.dot(exps.astype(BF16), value, preferred_element_type=F32)
    output = numerator / total
    spread = jnp.broadcast_to(peak + jnp.log(total), (2 * rows, LANES))
    return (
        jnp.where(first, output[:rows], output[rows:]),
        jnp.where(first, spread[:rows], spread[rows:]),
    )


def kernel(
    short_hbm, middle_hbm, global_hbm, q_hbm, k_hbm, v_hbm, w_hbm, o_ref, short_off, middle_off, global_off,
    q_in, k_in, v_in, w_in, plain, short_q, short_kv, short_out, middle_packets, global_packets, middle_in, global_in,
    role_q, gathered, role_out, results, merged, merged_rows, load_sem, send_sem, recv_sem, packet_send, packet_recv,
    result_send, result_recv, go_sem, row_sem,
):
    wide, narrow = lax.axis_index("wide"), lax.axis_index("narrow")
    x, y, c = narrow // 4, lax.rem(wide, 4), lax.rem(narrow, 2)
    z = lax.rem(narrow // 2, 2) * 4 + wide // 4
    z_hi = z // 4
    chip = x * 4 + y
    me = chip * 2 + c
    early = lax.rem(z // 2, 2) == 1

    def at(plane_place, to_z):
        to_chip = plane_place // 2
        return {
            "wide": lax.rem(to_z, 4) * 4 + lax.rem(to_chip, 4),
            "narrow": to_chip // 4 * 4 + to_z // 4 * 2 + lax.rem(plane_place, 2),
        }

    sibling = at(chip * 2 + 1 - c, z)

    def along_z(dz):
        return at(me, lax.rem(z + dz, Z_CHIPS))

    def send(source, target, send_to, recv_to, to):
        return pltpu.make_async_remote_copy(
            src_ref=source, dst_ref=target, send_sem=send_to, recv_sem=recv_to,
            device_id=to, device_id_type=MESH,
        )

    def to_sibling(i):
        return send(short_kv.at[i, 0], short_kv.at[i, 1], send_sem.at[SIBLING, i], recv_sem.at[SIBLING, i], sibling)

    def across(i):
        return send(short_kv.at[i, 0], short_kv.at[i, 2], send_sem.at[ACROSS, i], recv_sem.at[ACROSS, i], along_z(4))

    def pass_on(i):
        return send(short_kv.at[i, 2], short_kv.at[i, 3], send_sem.at[PASSED_ON, i], recv_sem.at[PASSED_ON, i], sibling)

    def worker(scope, tile):
        if scope == 0:
            return tile * 2
        return lax.rem(tile + GLOBAL_SHIFT, CHIPS) * 2 + 1

    own_tile = jnp.where(c == 0, chip, lax.rem(chip + CHIPS - GLOBAL_SHIFT, CHIPS))
    works = own_tile < TILES
    sibling_works = jnp.where(c == 0, chip >= GLOBAL_SHIFT, chip < TILES)

    def packet_to(scope, tile):
        source, target = ((middle_packets, middle_in), (global_packets, global_in))[scope]
        return send(
            source.at[tile], target.at[me], packet_send.at[scope, tile], packet_recv.at[me], at(worker(scope, tile), z)
        )

    def packet_from(scope, place):
        source, target = ((middle_packets, middle_in), (global_packets, global_in))[scope]
        return send(source.at[0], target.at[place], packet_send.at[scope, 0], packet_recv.at[place], at(place, z))

    def result_to(place):
        return send(
            role_out.at[place], results.at[c, own_tile], result_send.at[place], result_recv.at[c, own_tile], at(place, z)
        )

    def result_from(scope, tile):
        return send(
            role_out.at[0], results.at[scope, tile], result_send.at[0], result_recv.at[scope, tile],
            at(worker(scope, tile), z),
        )

    def middle_across():
        part = gathered.at[pl.ds(z_hi * 4, 4)]
        return send(part, part, send_sem.at[ALONG_Z, 4], recv_sem.at[ALONG_Z, 4], along_z(4))

    def global_to(dz):
        part = gathered.at[z]
        return send(part, part, send_sem.at[ALONG_Z, dz], recv_sem.at[ALONG_Z, dz], along_z(dz))

    barrier = pltpu.get_barrier_semaphore()

    def greet(to):
        pl.semaphore_signal(barrier, inc=1, device_id=to, device_id_type=MESH)

    greet(along_z(4))
    column = [
        at((x * 4 + lax.rem(y + dy, Y_CHIPS)) * 2 + lax.rem(c + dc, 2), z)
        for dy in range(Y_CHIPS) for dc in range(2) if dy or dc
    ]
    row = [at((lax.rem(x + dx, X_CHIPS) * 4 + y) * 2 + c, z) for dx in range(1, X_CHIPS)]
    for to in column + row:
        greet(to)

    @pl.when(c == 1)
    def _():
        for dz in (1, 2, 3, 5, 6, 7):
            greet(along_z(dz))

    loads = [
        pltpu.make_async_copy(source, target, load_sem.at[number])
        for number, (source, target) in enumerate((
            (short_hbm, short_off), (middle_hbm, middle_off), (global_hbm, global_off),
            (k_hbm, k_in), (v_hbm, v_in), (q_hbm, q_in), (w_hbm, w_in),
        ))
    ]
    for load in loads[:5]:
        load.start()

    first = first_head()

    def offsets(ref, i):
        return jnp.where(first, ref[2 * i], ref[2 * i + 1])

    def select_short(source, number, i):
        lanes = pl.ds(pl.multiple_of(i * LANES, LANES), LANES)
        plain[number] = source[:, lanes].astype(F32)
        even = plain[number, pl.ds(0, SHORT_ROWS, stride=2), :]
        odd = plain[number, pl.ds(1, SHORT_ROWS, stride=2), :]
        return jnp.where(offsets(short_off, i) == 0, even, odd).astype(BF16)

    for load in loads[:5]:
        load.wait()
    loads[5].start()

    @pl.loop(0, TILES)
    def _(i):
        short_kv[i, 0, 0] = select_short(k_in, 0, i)
        short_kv[i, 0, 1] = select_short(v_in, 1, i)

    pl.semaphore_wait(barrier, 1 + len(column) + len(row) + 6 * c)

    for to in row:
        pl.semaphore_signal(row_sem, inc=1, device_id=to, device_id_type=MESH)

    @pl.loop(0, jnp.where(early, AHEAD, 0))
    def _(i):
        across(i).start()

    loads[5].wait()

    @pl.loop(0, TILES)
    def _(i):
        lanes = pl.ds(pl.multiple_of(i * LANES, LANES), LANES)
        middle_at = offsets(middle_off, i)
        global_at = offsets(global_off, i)
        frame = lax.broadcasted_iota(jnp.int32, (FRAMES, LANES), 0)
        in_middle = lax.rem(frame, 32) == middle_at
        in_global = lax.rem(frame, 128) == global_at
        eight = lax.broadcasted_iota(jnp.int32, (8, LANES), 0)
        rows = []
        last = jnp.zeros((8, LANES), F32)
        for number, source in enumerate((q_in, k_in, v_in)):
            values = source[:, lanes].astype(F32)
            rows.append(jnp.sum(jnp.where(in_middle, values, 0.0).reshape(MIDDLE_ROWS, 32, LANES), axis=1))
            global_rows = jnp.sum(jnp.where(in_global, values, 0.0).reshape(GLOBAL_ROWS, 128, LANES), axis=1)
            for row in range(GLOBAL_ROWS):
                last = jnp.where(eight == 2 * number + row, global_rows[row : row + 1], last)
        middle_packets[i] = jnp.concatenate([*rows, jnp.zeros((8, LANES), F32)], axis=0).astype(BF16)
        global_packets[i] = jnp.concatenate([last, jnp.zeros((8, LANES), F32)], axis=0).astype(BF16)

    pl.semaphore_wait(row_sem, len(row))

    @pl.loop(0, TILES)
    def _(step):
        tile = lax.rem(step + me, TILES)
        for scope, (source, target) in enumerate(((middle_packets, middle_in), (global_packets, global_in))):
            @pl.when(worker(scope, tile) != me)
            def _():
                packet_to(scope, tile).start()

            @pl.when(worker(scope, tile) == me)
            def _():
                target[me] = source[tile]

    loads[6].start()

    @pl.loop(0, TILES)
    def _(i):
        to_sibling(i).start()
        short_q[i] = select_short(q_in, 2, i)

    def pick(shape, place):
        row = lax.broadcasted_iota(jnp.int32, shape, 0)
        column = lax.broadcasted_iota(jnp.int32, shape, 1)
        return jnp.where(column == place(row), 1.0, 0.0).astype(BF16)

    def take(one_hot, rows):
        return jnp.dot(one_hot, rows, preferred_element_type=F32).astype(BF16)

    @pl.when(works & (c == 0))
    def _():
        @pl.loop(1, PLANE)
        def _(step):
            packet_from(0, lax.rem(me + step, PLANE)).wait_recv()

        def place(first_row):
            return lambda row: row // 8 * MIDDLE_PACKET + first_row + lax.rem(row, 8)

        picks = [pick((64, BLOCK * MIDDLE_PACKET), place(first_row)) for first_row in (0, 8, 16)]

        @pl.loop(0, BLOCKS)
        def _(block):
            rows = middle_in[pl.ds(block * BLOCK, BLOCK)].reshape(BLOCK * MIDDLE_PACKET, LANES)
            role_q[block] = take(picks[0], rows)
            for part in range(2):
                gathered[z_hi * 4 + block, part] = take(picks[1 + part], rows)

        middle_across().start()

    @pl.when(works & (c == 1))
    def _():
        @pl.loop(1, PLANE)
        def _(step):
            packet_from(1, lax.rem(me + step, PLANE)).wait_recv()

        def place_query(row):
            within = lax.rem(row, 8)
            return jnp.where(within < GLOBAL_ROWS, row // 8 * GLOBAL_PACKET + within, -1)

        def place(first_row):
            return lambda row: row // 2 * GLOBAL_PACKET + first_row + lax.rem(row, 2)

        rows = global_in[...].reshape(PLANE * GLOBAL_PACKET, LANES)
        for part in range(2):
            gathered[z, part] = take(pick((64, PLANE * GLOBAL_PACKET), place(2 + 2 * part)), rows)
        for dz in range(1, Z_CHIPS):
            global_to(dz).start()
        query_pick = pick((64, BLOCK * GLOBAL_PACKET), place_query)

        @pl.loop(0, BLOCKS)
        def _(block):
            role_q[block] = take(
                query_pick, global_in[pl.ds(block * BLOCK, BLOCK)].reshape(BLOCK * GLOBAL_PACKET, LANES)
            )

    @pl.loop(jnp.where(early, TILES, 0), TILES)
    def _(i):
        across(i).start()

    def wait_along_z():
        @pl.when(works & (c == 0))
        def _():
            middle_across().wait_recv()

        @pl.when(works & (c == 1))
        def _():
            for dz in range(1, Z_CHIPS):
                global_to(dz).wait_recv()

        @pl.when(early & works & ~sibling_works)
        def _():
            pl.semaphore_signal(go_sem, inc=1, device_id=sibling, device_id_type=MESH)

        @pl.when(early & ~works)
        def _():
            pl.semaphore_wait(go_sem, 1)

        @pl.loop(jnp.where(early, AHEAD, TILES), TILES)
        def _(i):
            across(i).start()

    def work():
        key = gathered[:, 0].reshape(KEPT_ROWS, LANES)
        value = gathered[:, 1].reshape(KEPT_ROWS, LANES)

        @pl.loop(0, BLOCKS)
        def _(block):
            output, spread = attend(role_q[block], key, value)
            places = pl.ds(block * BLOCK, BLOCK)
            role_out[places, 0] = output.reshape(BLOCK, 8, LANES)
            role_out[places, 1] = spread.reshape(BLOCK, 8, LANES)

        @pl.loop(1, PLANE)
        def _(step):
            result_to(lax.rem(me + step, PLANE)).start()

        results[c, own_tile] = role_out[me]

    def short_scope(i):
        to_sibling(i).wait_recv()
        pass_on(i).wait_recv()
        output, spread = attend(
            short_q[i],
            short_kv[i, :, 0].reshape(KEPT_ROWS, LANES),
            short_kv[i, :, 1].reshape(KEPT_ROWS, LANES),
        )
        short_out[i, 0] = output
        short_out[i, 1] = spread

    def finish(i):
        short_at, middle_at, global_at = (offsets(ref, i) for ref in (short_off, middle_off, global_off))
        for parity in range(2):
            shape = (SHORT_ROWS, LANES)
            row = lax.broadcasted_iota(jnp.int32, shape, 0)
            covers = (
                jnp.broadcast_to(short_at == parity, shape),
                2 * lax.rem(row, 16) + parity == middle_at,
                2 * lax.rem(row, 64) + parity == global_at,
            )

            def spread_out(value, count):
                return jnp.broadcast_to(
                    value[:count].reshape(count, 1, LANES), (count, SHORT_ROWS // count, LANES)
                ).reshape(shape)

            outs = (
                short_out[i, 0],
                spread_out(results[0, i, 0], MIDDLE_ROWS),
                spread_out(results[1, i, 0], GLOBAL_ROWS),
            )
            spreads = (
                short_out[i, 1],
                spread_out(results[0, i, 1], MIDDLE_ROWS),
                spread_out(results[1, i, 1], GLOBAL_ROWS),
            )
            masked = [jnp.where(cover, value, MASKED) for cover, value in zip(covers, spreads)]
            top = jnp.maximum(jnp.maximum(masked[0], masked[1]), masked[2])
            weights = [jnp.where(cover, jnp.exp(value - top), 0.0) for cover, value in zip(covers, masked)]
            denominator = weights[0] + weights[1] + weights[2]
            denominator = jnp.where(denominator == 0.0, 1.0, denominator)
            total = weights[0] * outs[0] + weights[1] * outs[1] + weights[2] * outs[2]
            merged[pl.ds(parity, SHORT_ROWS, stride=2), :] = total / denominator
        merged_rows[:, pl.ds(pl.multiple_of(i * LANES, LANES), LANES)] = merged[...].astype(BF16)

    def project(first_tile, end_tile):
        depth = pl.ds(first_tile * LANES, (end_tile - first_tile) * LANES)
        for part in range(6):
            columns = pl.ds(part * 256, 256)
            product = jnp.dot(merged_rows[:, depth], w_in[depth, columns], preferred_element_type=F32)
            if first_tile:
                product += o_ref[:, columns]
            o_ref[:, columns] = product

    def wait_results():
        @pl.loop(0, TILES)
        def _(tile):
            for scope in range(2):
                @pl.when(worker(scope, tile) != me)
                def _():
                    result_from(scope, tile).wait_recv()

    def sent(i):
        to_sibling(i).wait_send()
        across(i).wait_send()
        pass_on(i).wait_send()

    def sent_rows():
        @pl.loop(0, TILES)
        def _(i):
            for scope in range(2):
                @pl.when(worker(scope, i) != me)
                def _():
                    packet_to(scope, i).wait_send()

        @pl.when(works)
        def _():
            @pl.loop(1, PLANE)
            def _(step):
                result_to(lax.rem(me + step, PLANE)).wait_send()

            @pl.when(c == 0)
            def _():
                middle_across().wait_send()

            @pl.when(c == 1)
            def _():
                for dz in range(1, Z_CHIPS):
                    global_to(dz).wait_send()

    merge_tile = jnp.where(early, AHEAD, 0)

    @pl.loop(0, TILES + 1)
    def _(i):
        @pl.when(i == merge_tile)
        def _():
            wait_along_z()

        @pl.when((i == merge_tile) & works)
        def _():
            work()

        @pl.when(i < TILES)
        def _():
            across(i).wait_recv()
            pass_on(i).start()

        @pl.when(i > 0)
        def _():
            short_scope(i - 1)

        @pl.when(i == FINISH_TILE)
        def _():
            wait_results()
            loads[6].wait()

        @pl.when(i >= FINISH_TILE)
        def _():
            @pl.loop(jnp.where(i == FINISH_TILE, 0, i - 1), i)
            def _(tile):
                finish(tile)

        for first_tile, end_tile in zip(PROJECTED, PROJECTED[1:]):
            @pl.when(i == end_tile)
            def _():
                project(first_tile, end_tile)

        @pl.when(i > 1)
        def _():
            sent(i - 2)

        @pl.when(i == 9)
        def _():
            sent_rows()

    sent(TILES - 1)


def per_device(queries, keys, values, short_offsets, middle_offsets, global_offsets, w_out):
    frames, width = queries.shape
    heads = short_offsets.shape
    return pl.pallas_call(
        kernel,
        out_shape=pltpu.VMEM((frames, width), F32),
        in_specs=[pl.BlockSpec(memory_space=pltpu.HBM)] * 7,
        out_specs=pl.BlockSpec(memory_space=pltpu.VMEM),
        scratch_shapes=[
            pltpu.SMEM(heads, jnp.int32),
            pltpu.SMEM(heads, jnp.int32),
            pltpu.SMEM(heads, jnp.int32),
            pltpu.VMEM((frames, width), BF16),
            pltpu.VMEM((frames, width), BF16),
            pltpu.VMEM((frames, width), BF16),
            pltpu.VMEM((width, width), BF16),
            pltpu.VMEM((3, frames, LANES), F32),
            pltpu.VMEM((TILES, SHORT_ROWS, LANES), BF16),
            pltpu.VMEM((TILES, 4, 2, SHORT_ROWS, LANES), BF16),
            pltpu.VMEM((TILES, 2, SHORT_ROWS, LANES), F32),
            pltpu.VMEM((TILES, MIDDLE_PACKET, LANES), BF16),
            pltpu.VMEM((TILES, GLOBAL_PACKET, LANES), BF16),
            pltpu.VMEM((PLANE, MIDDLE_PACKET, LANES), BF16),
            pltpu.VMEM((PLANE, GLOBAL_PACKET, LANES), BF16),
            pltpu.VMEM((BLOCKS, 64, LANES), BF16),
            pltpu.VMEM((8, 2, 64, LANES), BF16),
            pltpu.VMEM((PLANE, 2, 8, LANES), F32),
            pltpu.VMEM((2, TILES, 2, 8, LANES), F32),
            pltpu.VMEM((frames, LANES), F32),
            pltpu.VMEM((frames, width), BF16),
            pltpu.SemaphoreType.DMA((7,)),
            pltpu.SemaphoreType.DMA((4, TILES)),
            pltpu.SemaphoreType.DMA((4, TILES)),
            pltpu.SemaphoreType.DMA((2, TILES)),
            pltpu.SemaphoreType.DMA((PLANE,)),
            pltpu.SemaphoreType.DMA((PLANE,)),
            pltpu.SemaphoreType.DMA((2, TILES)),
            pltpu.SemaphoreType.REGULAR,
            pltpu.SemaphoreType.REGULAR,
        ],
        compiler_params=pltpu.CompilerParams(
            collective_id=0, has_side_effects=True, vmem_limit_bytes=60 * 1024 * 1024
        ),
        name="dilated_attention",
    )(short_offsets, middle_offsets, global_offsets, queries, keys, values, w_out)


def solution(mesh):
    placed = (
        P(("wide", "narrow"), None),
        P(("wide", "narrow"), None),
        P(("wide", "narrow"), None),
        P(),
        P(),
        P(),
        P(),
    )
    return jax.shard_map(
        per_device,
        mesh=mesh,
        in_specs=placed,
        out_specs=P(("wide", "narrow"), None),
        check_vma=False,
    )
```

time: 80.4 us -> 56.5 us (0.70)
  the two profiles are of different devices: /device:TPU:1 before, /device:TPU:67 now
where the time goes in v2:
time: 56.5 us; the launch traced here: 56.3 us
  Pallas kernels  55.2 us (98%)
  local copies, waits for them, and re-layouts  1.15 us (2%)
    pallas_call x1, Pallas kernels, per_device(): pl.pallas_call(kernel, out_shape=pltpu.VMEM((frames, width), F32), in_spe...  55.2 us
    unnamed x1, local copies, waits for them, and re-layouts  1.15 us

profile of v2, /device:TPU:67, one launch (start us, length us, event | category | flops | bytes accessed | tf_op | source)
XLA Modules:
  0.0 56.3 jit_solution(808279408102687501)
XLA Ops:
  0.0 55.2 %dilated_attention.1 = f32[256,1536]{1,0:T(8,128)S(1)} custom-call(s32[24]{0:T(128)} %short_hbm.1, s32[24]{0:T(128)} %middle_hbm.1, s32[24]{0:T(128)} %global_hbm.1, bf16[256,1536]{1,0:T(8,128)(2,1)} %q_hbm.1, bf16[256,1536]{1,0:T(8,128)(2,1)} %k_hbm.1, bf16[256,1536]{1,0:T(8,128)(2,1)} %v_hbm.1, bf16[1536,1536]{1,0:T(8,128)(2,1)} %w_hbm.1), custom_call_target="tpu_custom_call" | custom-call | tf_op jit(solution)/shard_map/dilated_attention/pallas_call | solution.py:481
  55.2 1.1 %copy.9 = f32[256,1536]{1,0:T(8,128)} copy(f32[256,1536]{1,0:T(8,128)S(1)} %dilated_attention.1) | data formatting | bytes 3145728

commit v3 on v2

--- a/solution.py
+++ b/solution.py
@@ -25,9 +25,8 @@
 BLOCK = 8
 BLOCKS = PLANE // BLOCK
 GLOBAL_SHIFT = 4
-AHEAD = 6
 FINISH_TILE = 6
-PROJECTED = (0, FINISH_TILE, 9, 11, 12)
+PROJECTED = (0, FINISH_TILE, 10, 12)
 MASKED = -1e30
 
 SIBLING, ACROSS, PASSED_ON, ALONG_Z = range(4)
@@ -62,7 +61,7 @@
     short_hbm, middle_hbm, global_hbm, q_hbm, k_hbm, v_hbm, w_hbm, o_ref, short_off, middle_off, global_off,
     q_in, k_in, v_in, w_in, plain, short_q, short_kv, short_out, middle_packets, global_packets, middle_in, global_in,
     role_q, gathered, role_out, results, merged, merged_rows, load_sem, send_sem, recv_sem, packet_send, packet_recv,
-    result_send, result_recv, go_sem, row_sem,
+    result_send, result_recv, row_sem,
 ):
     wide, narrow = lax.axis_index("wide"), lax.axis_index("narrow")
     x, y, c = narrow // 4, lax.rem(wide, 4), lax.rem(narrow, 2)
@@ -70,13 +69,13 @@
     z_hi = z // 4
     chip = x * 4 + y
     me = chip * 2 + c
-    early = lax.rem(z // 2, 2) == 1
+    early = lax.rem(z // 2, 2) == 0
 
     def at(plane_place, to_z):
-        to_chip = plane_place // 2
+        to_chip = lax.div(plane_place, 2)
         return {
             "wide": lax.rem(to_z, 4) * 4 + lax.rem(to_chip, 4),
-            "narrow": to_chip // 4 * 4 + to_z // 4 * 2 + lax.rem(plane_place, 2),
+            "narrow": lax.div(to_chip, 4) * 4 + lax.div(to_z, 4) * 2 + lax.rem(plane_place, 2),
         }
 
     sibling = at(chip * 2 + 1 - c, z)
@@ -106,7 +105,6 @@
 
     own_tile = jnp.where(c == 0, chip, lax.rem(chip + CHIPS - GLOBAL_SHIFT, CHIPS))
     works = own_tile < TILES
-    sibling_works = jnp.where(c == 0, chip >= GLOBAL_SHIFT, chip < TILES)
 
     def packet_to(scope, tile):
         source, target = ((middle_packets, middle_in), (global_packets, global_in))[scope]
@@ -136,25 +134,6 @@
     def global_to(dz):
         part = gathered.at[z]
         return send(part, part, send_sem.at[ALONG_Z, dz], recv_sem.at[ALONG_Z, dz], along_z(dz))
-
-    barrier = pltpu.get_barrier_semaphore()
-
-    def greet(to):
-        pl.semaphore_signal(barrier, inc=1, device_id=to, device_id_type=MESH)
-
-    greet(along_z(4))
-    column = [
-        at((x * 4 + lax.rem(y + dy, Y_CHIPS)) * 2 + lax.rem(c + dc, 2), z)
-        for dy in range(Y_CHIPS) for dc in range(2) if dy or dc
-    ]
-    row = [at((lax.rem(x + dx, X_CHIPS) * 4 + y) * 2 + c, z) for dx in range(1, X_CHIPS)]
-    for to in column + row:
-        greet(to)
-
-    @pl.when(c == 1)
-    def _():
-        for dz in (1, 2, 3, 5, 6, 7):
-            greet(along_z(dz))
 
     loads = [
         pltpu.make_async_copy(source, target, load_sem.at[number])
@@ -166,6 +145,25 @@
     for load in loads[:5]:
         load.start()
 
+    barrier = pltpu.get_barrier_semaphore()
+
+    def greet(to):
+        pl.semaphore_signal(barrier, inc=1, device_id=to, device_id_type=MESH)
+
+    greet(along_z(4))
+    column = [
+        at((x * 4 + lax.rem(y + dy, Y_CHIPS)) * 2 + lax.rem(c + dc, 2), z)
+        for dy in range(Y_CHIPS) for dc in range(2) if dy or dc
+    ]
+    row = [at((lax.rem(x + dx, X_CHIPS) * 4 + y) * 2 + c, z) for dx in range(1, X_CHIPS)]
+    for to in column + row:
+        greet(to)
+
+    @pl.when(c == 1)
+    def _():
+        for dz in (1, 2, 3, 5, 6, 7):
+            greet(along_z(dz))
+
     first = first_head()
 
     def offsets(ref, i):
@@ -192,20 +190,29 @@
     for to in row:
         pl.semaphore_signal(row_sem, inc=1, device_id=to, device_id_type=MESH)
 
-    @pl.loop(0, jnp.where(early, AHEAD, 0))
+    @pl.loop(0, jnp.where(early, TILES, 0))
     def _(i):
         across(i).start()
 
     loads[5].wait()
+    loads[6].start()
 
     @pl.loop(0, TILES)
     def _(i):
+        to_sibling(i).start()
+        short_q[i] = select_short(q_in, 2, i)
+
+    pl.semaphore_wait(row_sem, len(row))
+
+    @pl.loop(0, TILES)
+    def _(step):
+        i = lax.rem(step + me, TILES)
         lanes = pl.ds(pl.multiple_of(i * LANES, LANES), LANES)
         middle_at = offsets(middle_off, i)
         global_at = offsets(global_off, i)
         frame = lax.broadcasted_iota(jnp.int32, (FRAMES, LANES), 0)
-        in_middle = lax.rem(frame, 32) == middle_at
-        in_global = lax.rem(frame, 128) == global_at
+        in_middle = frame & 31 == middle_at
+        in_global = frame & 127 == global_at
         eight = lax.broadcasted_iota(jnp.int32, (8, LANES), 0)
         rows = []
         last = jnp.zeros((8, LANES), F32)
@@ -218,26 +225,14 @@
         middle_packets[i] = jnp.concatenate([*rows, jnp.zeros((8, LANES), F32)], axis=0).astype(BF16)
         global_packets[i] = jnp.concatenate([last, jnp.zeros((8, LANES), F32)], axis=0).astype(BF16)
 
-    pl.semaphore_wait(row_sem, len(row))
-
-    @pl.loop(0, TILES)
-    def _(step):
-        tile = lax.rem(step + me, TILES)
         for scope, (source, target) in enumerate(((middle_packets, middle_in), (global_packets, global_in))):
-            @pl.when(worker(scope, tile) != me)
+            @pl.when(worker(scope, i) != me)
             def _():
-                packet_to(scope, tile).start()
-
-            @pl.when(worker(scope, tile) == me)
+                packet_to(scope, i).start()
+
+            @pl.when(worker(scope, i) == me)
             def _():
-                target[me] = source[tile]
-
-    loads[6].start()
-
-    @pl.loop(0, TILES)
-    def _(i):
-        to_sibling(i).start()
-        short_q[i] = select_short(q_in, 2, i)
+                target[me] = source[i]
 
     def pick(shape, place):
         row = lax.broadcasted_iota(jnp.int32, shape, 0)
@@ -254,7 +249,7 @@
             packet_from(0, lax.rem(me + step, PLANE)).wait_recv()
 
         def place(first_row):
-            return lambda row: row // 8 * MIDDLE_PACKET + first_row + lax.rem(row, 8)
+            return lambda row: (row >> 3) * MIDDLE_PACKET + first_row + (row & 7)
 
         picks = [pick((64, BLOCK * MIDDLE_PACKET), place(first_row)) for first_row in (0, 8, 16)]
 
@@ -274,11 +269,11 @@
             packet_from(1, lax.rem(me + step, PLANE)).wait_recv()
 
         def place_query(row):
-            within = lax.rem(row, 8)
-            return jnp.where(within < GLOBAL_ROWS, row // 8 * GLOBAL_PACKET + within, -1)
+            within = row & 7
+            return jnp.where(within < GLOBAL_ROWS, (row >> 3) * GLOBAL_PACKET + within, -1)
 
         def place(first_row):
-            return lambda row: row // 2 * GLOBAL_PACKET + first_row + lax.rem(row, 2)
+            return lambda row: (row >> 1) * GLOBAL_PACKET + first_row + (row & 1)
 
         rows = global_in[...].reshape(PLANE * GLOBAL_PACKET, LANES)
         for part in range(2):
@@ -306,18 +301,6 @@
         def _():
             for dz in range(1, Z_CHIPS):
                 global_to(dz).wait_recv()
-
-        @pl.when(early & works & ~sibling_works)
-        def _():
-            pl.semaphore_signal(go_sem, inc=1, device_id=sibling, device_id_type=MESH)
-
-        @pl.when(early & ~works)
-        def _():
-            pl.semaphore_wait(go_sem, 1)
-
-        @pl.loop(jnp.where(early, AHEAD, TILES), TILES)
-        def _(i):
-            across(i).start()
 
     def work():
         key = gathered[:, 0].reshape(KEPT_ROWS, LANES)
@@ -354,8 +337,8 @@
             row = lax.broadcasted_iota(jnp.int32, shape, 0)
             covers = (
                 jnp.broadcast_to(short_at == parity, shape),
-                2 * lax.rem(row, 16) + parity == middle_at,
-                2 * lax.rem(row, 64) + parity == global_at,
+                2 * (row & 15) + parity == middle_at,
+                2 * (row & 63) + parity == global_at,
             )
 
             def spread_out(value, count):
@@ -427,7 +410,8 @@
                 for dz in range(1, Z_CHIPS):
                     global_to(dz).wait_send()
 
-    merge_tile = jnp.where(early, AHEAD, 0)
+    merge_tile = jnp.where(early, TILES, 0)
+    finish_tile = jnp.where(early, TILES, FINISH_TILE)
 
     @pl.loop(0, TILES + 1)
     def _(i):
@@ -439,6 +423,11 @@
         def _():
             work()
 
+        @pl.when(i == finish_tile)
+        def _():
+            wait_results()
+            loads[6].wait()
+
         @pl.when(i < TILES)
         def _():
             across(i).wait_recv()
@@ -448,27 +437,26 @@
         def _():
             short_scope(i - 1)
 
-        @pl.when(i == FINISH_TILE)
-        def _():
-            wait_results()
-            loads[6].wait()
-
-        @pl.when(i >= FINISH_TILE)
-        def _():
-            @pl.loop(jnp.where(i == FINISH_TILE, 0, i - 1), i)
+        @pl.when(i >= finish_tile)
+        def _():
+            @pl.loop(jnp.where(i == finish_tile, 0, i - 1), i)
             def _(tile):
                 finish(tile)
 
         for first_tile, end_tile in zip(PROJECTED, PROJECTED[1:]):
-            @pl.when(i == end_tile)
+            @pl.when((i == end_tile) & ~early)
             def _():
                 project(first_tile, end_tile)
 
+        @pl.when((i == TILES) & early)
+        def _():
+            project(0, TILES)
+
         @pl.when(i > 1)
         def _():
             sent(i - 2)
 
-        @pl.when(i == 9)
+        @pl.when(i == jnp.where(early, TILES, 9))
         def _():
             sent_rows()
 
@@ -513,7 +501,6 @@
             pltpu.SemaphoreType.DMA((PLANE,)),
             pltpu.SemaphoreType.DMA((2, TILES)),
             pltpu.SemaphoreType.REGULAR,
-            pltpu.SemaphoreType.REGULAR,
         ],
         compiler_params=pltpu.CompilerParams(
             collective_id=0, has_side_effects=True, vmem_limit_bytes=60 * 1024 * 1024

time: 56.5 us -> 55.5 us (0.982)
  Pallas kernels: 55.2 us -> 54.3 us
    pallas_call x1, Pallas kernels: 55.2 us -> 54.3 us  [per_device(): pl.pallas_call(kernel, out_shape=pltpu.VMEM((frames, width), F32), in_spe...]
where the time goes in v3:
time: 55.5 us; the launch traced here: 55.4 us
  Pallas kernels  54.3 us (98%)
  local copies, waits for them, and re-layouts  1.15 us (2%)
    pallas_call x1, Pallas kernels, per_device(): pl.pallas_call(kernel, out_shape=pltpu.VMEM((frames, width), F32), in_spe...  54.3 us
    unnamed x1, local copies, waits for them, and re-layouts  1.15 us

profile of v3, /device:TPU:67, one launch (start us, length us, event | category | flops | bytes accessed | tf_op | source)
XLA Modules:
  0.0 55.4 jit_solution(14937741704605347700)
XLA Ops:
  0.0 54.3 %dilated_attention.1 = f32[256,1536]{1,0:T(8,128)S(1)} custom-call(s32[24]{0:T(128)} %short_hbm.1, s32[24]{0:T(128)} %middle_hbm.1, s32[24]{0:T(128)} %global_hbm.1, bf16[256,1536]{1,0:T(8,128)(2,1)} %q_hbm.1, bf16[256,1536]{1,0:T(8,128)(2,1)} %k_hbm.1, bf16[256,1536]{1,0:T(8,128)(2,1)} %v_hbm.1, bf16[1536,1536]{1,0:T(8,128)(2,1)} %w_hbm.1), custom_call_target="tpu_custom_call" | custom-call | tf_op jit(solution)/shard_map/dilated_attention/pallas_call | solution.py:469
  54.3 1.1 %copy.9 = f32[256,1536]{1,0:T(8,128)} copy(f32[256,1536]{1,0:T(8,128)S(1)} %dilated_attention.1) | data formatting | bytes 3145728

commit v4 on v3

--- a/solution.py
+++ b/solution.py
@@ -135,6 +135,12 @@
         part = gathered.at[z]
         return send(part, part, send_sem.at[ALONG_Z, dz], recv_sem.at[ALONG_Z, dz], along_z(dz))
 
+    barrier = pltpu.get_barrier_semaphore()
+
+    def greet(to):
+        pl.semaphore_signal(barrier, inc=1, device_id=to, device_id_type=MESH)
+
+    greet(along_z(4))
     loads = [
         pltpu.make_async_copy(source, target, load_sem.at[number])
         for number, (source, target) in enumerate((
@@ -145,12 +151,7 @@
     for load in loads[:5]:
         load.start()
 
-    barrier = pltpu.get_barrier_semaphore()
-
-    def greet(to):
-        pl.semaphore_signal(barrier, inc=1, device_id=to, device_id_type=MESH)
-
-    greet(along_z(4))
+
     column = [
         at((x * 4 + lax.rem(y + dy, Y_CHIPS)) * 2 + lax.rem(c + dc, 2), z)
         for dy in range(Y_CHIPS) for dc in range(2) if dy or dc

time: 55.5 us -> 55.5 us (level)
  no operation moved by 1% of the time
where the time goes in v4:
time: 55.5 us; the launch traced here: 55.4 us
  Pallas kernels  54.3 us (98%)
  local copies, waits for them, and re-layouts  1.15 us (2%)
    pallas_call x1, Pallas kernels, per_device(): pl.pallas_call(kernel, out_shape=pltpu.VMEM((frames, width), F32), in_spe...  54.3 us
    unnamed x1, local copies, waits for them, and re-layouts  1.15 us

profile of v4, /device:TPU:67, one launch (start us, length us, event | category | flops | bytes accessed | tf_op | source)
XLA Modules:
  0.0 55.4 jit_solution(6100744460739337191)
XLA Ops:
  0.0 54.3 %dilated_attention.1 = f32[256,1536]{1,0:T(8,128)S(1)} custom-call(s32[24]{0:T(128)} %short_hbm.1, s32[24]{0:T(128)} %middle_hbm.1, s32[24]{0:T(128)} %global_hbm.1, bf16[256,1536]{1,0:T(8,128)(2,1)} %q_hbm.1, bf16[256,1536]{1,0:T(8,128)(2,1)} %k_hbm.1, bf16[256,1536]{1,0:T(8,128)(2,1)} %v_hbm.1, bf16[1536,1536]{1,0:T(8,128)(2,1)} %w_hbm.1), custom_call_target="tpu_custom_call" | custom-call | tf_op jit(solution)/shard_map/dilated_attention/pallas_call | solution.py:470
  54.3 1.1 %copy.9 = f32[256,1536]{1,0:T(8,128)} copy(f32[256,1536]{1,0:T(8,128)S(1)} %dilated_attention.1) | data formatting | bytes 3145728
